TPU v7x, 128 devices: a whole 4x4x4 slice. The times are simulated.
128 devices in a mesh: gx: 32 (over z_hi, x, y), gy: 4 (over z_lo, core).
Axes of the slice: x: 4, y: 4, z: 4 (z_hi: 2, z_lo: 2; z = z_hi * 2 + z_lo), core: 2. Of those that a mesh axis runs over, the one named last changes fastest.
Arguments:
- populations: float32 [27, 256, 64, 512], P(None, 'gx', 'gy'), as said below
- solid: int32 [256, 64, 512], P('gx', 'gy'), may hold values 0 or 1
- basis: float32 [64, 3, 256, 4096], P(None, None, ('gx', 'gy'))
- singular: float32 [64], replicated, may hold values from 0.5 to 20
- recent: float32 [7, 3, 256, 4096], P(None, None, ('gx', 'gy'))
- age: int32 [8], replicated, may hold values from 0 to 7
Outputs:
- next_populations: float32 [27, 256, 64, 512], P(None, 'gx', 'gy')
- directions: float32 [8, 3, 256, 4096], P(None, None, ('gx', 'gy'))
- core: float32 [72, 72], replicated
Inputs may be any that keep to these rules, and one draw needn't show every extreme that they name: `populations`: every population is positive.
All inputs are finite; a program needn't handle non-finite values. No bound on the sum of `solid` on one device may be relied on, other than what follows from the above.
Results may differ from a plain program's by a relative error of at most 0.0003.
Values sent between devices are 32-bit elements; how exact they have to be, the bound alone decides.
A program may use at most 128 MiB of HBM per device.

v0:
```python
import functools

import jax
import jax.numpy as jnp
from jax import lax
from jax.experimental import pallas as pl
from jax.experimental.pallas import tpu as pltpu
from jax.sharding import PartitionSpec as P

MESH = pl.DeviceIdType.MESH
HIGHEST = lax.Precision.HIGHEST
omega_rate = 1.0 / 0.6
keep_rate = 1.0 - omega_rate
vel_gain = 50.0
age_span = 8.0
WEIGHTS = (8.0 / 27.0, 2.0 / 27.0, 1.0 / 54.0, 1.0 / 216.0)
NDEV = 128
RANK = 64
SNAPS = 8
ROWS = 192
TOTAL = 3145728.0


def direction(i):
    return i // 9 - 1, i // 3 % 3 - 1, i % 3 - 1


def shifted(value, shift_y, shift_z):
    if shift_z:
        value = pltpu.roll(value, 1 if shift_z > 0 else value.shape[1] - 1, 1)
    if shift_y:
        value = pltpu.roll(value, 1 if shift_y > 0 else value.shape[0] - 1, 0)
    return value


def collide_plane(x, pops, solid, mo, nxt):
    for piece in range(4):
        lanes = pl.ds(piece * 128, 128)
        total = [None] * 4
        for e in range(3):
            row = [None] * 3
            for f in range(3):
                p0, p1, p2 = (pops[9 * e + 3 * f + g, x, :, lanes] for g in range(3))
                row[f] = (p0 + p1 + p2, p2 - p0)
            dens = row[0][0] + row[1][0] + row[2][0]
            my = row[2][0] - row[0][0]
            mz = row[0][1] + row[1][1] + row[2][1]
            if e == 0:
                total = [dens, -dens, my, mz]
            else:
                total = [
                    total[0] + dens,
                    total[1] + dens if e == 2 else total[1],
                    total[2] + my,
                    total[3] + mz,
                ]
        inv = 1.0 / total[0]
        ux, uy, uz = total[1] * inv, total[2] * inv, total[3] * inv
        scaled = omega_rate * total[0]
        mo[0, :, lanes] = scaled
        mo[1, :, lanes] = ux
        mo[2, :, lanes] = uy
        mo[3, :, lanes] = uz
        mo[4, :, lanes] = scaled * (1.0 - 1.5 * (ux * ux + uy * uy + uz * uz))

    x_up, x_down = lax.rem(x + 1, 8), lax.rem(x + 7, 8)
    place = {0: x, 1: x_up, -1: x_down}
    for pos in range(14, 27):
        neg = 26 - pos
        ex, ey, ez = direction(pos)
        weight = WEIGHTS[abs(ex) + abs(ey) + abs(ez)]
        along = None
        for axis, part in enumerate((ex, ey, ez)):
            if part:
                term = mo[1 + axis]
                if along is None:
                    along = term if part > 0 else -term
                else:
                    along = along + term if part > 0 else along - term
        is_solid = solid[x] > 0
        scaled = mo[0] * along
        even = weight * mo[4] + (4.5 * weight) * (scaled * along)
        odd = (3.0 * weight) * scaled
        p_pos, p_neg = pops[pos, x], pops[neg, x]
        r_pos = jnp.where(is_solid, p_neg, keep_rate * p_pos + (even + odd))
        r_neg = jnp.where(is_solid, p_pos, keep_rate * p_neg + (even - odd))
        nxt[ex + 1, ey + 1, ez + 1, place[ex]] = shifted(r_pos, ey, ez)
        nxt[1 - ex, 1 - ey, 1 - ez, place[-ex]] = shifted(r_neg, -ey, -ez)
    still = pops[13, x]
    nxt[1, 1, 1, x] = jnp.where(solid[x] > 0, still, keep_rate * still + WEIGHTS[0] * mo[4])


def plane_sums(nxt, plane, firsts, lanes):
    inner, outer = None, None
    for e in firsts:
        row = []
        for f in range(3):
            p0, p1, p2 = (nxt[e, f, g, plane, :, lanes] for g in range(3))
            row.append((p0 + p1 + p2, p2 - p0))
        dens = row[0][0] + row[1][0]
        now_in = [dens, (e - 1) * dens if e != 1 else None, -row[0][0], row[0][1] + row[1][1]]
        now_out = [row[2][0], (e - 1) * row[2][0] if e != 1 else None, row[2][0], row[2][1]]
        if inner is None:
            inner, outer = now_in, now_out
        else:
            inner = [a if b is None else b if a is None else a + b for a, b in zip(inner, now_in)]
            outer = [a if b is None else b if a is None else a + b for a, b in zip(outer, now_out)]
    return inner, outer


def main_kernel(
    pops_in, solid_in, modes_in, recent_in, age_in,
    nxt, resid, small,
    pops, solid, modes, snaps, mo, sums, mxw, mxs, mxr, mys, myr, mcs, mcr,
    field, turned, parcel, arrived, xr_up, xr_dn, yr_up, yr_dn, corner,
    stack, mine1, got1, mine2, got2, mine3, got3, spread,
    load_sem, small_ssem, small_rsem, bulk_ssem, bulk_rsem, ex_ssem, ex_rsem, fix_sem,
):
    gx, gy = lax.axis_index("gx"), lax.axis_index("gy")
    me = gx * 4 + gy
    gx_up, gx_dn = lax.rem(gx + 1, 32), lax.rem(gx + 31, 32)
    gy_up, gy_dn = lax.rem(gy + 1, 4), lax.rem(gy + 3, 4)

    solid_copy = pltpu.make_async_copy(solid_in, solid, load_sem.at[8])
    solid_copy.start()

    def plane_copy(x):
        return pltpu.make_async_copy(pops_in.at[:, x], pops.at[:, x], load_sem.at[x])

    for x in (7, 0, 1, 2, 3, 4, 5, 6):
        plane_copy(x).start()
    recent_copy = pltpu.make_async_copy(recent_in, snaps.at[pl.ds(ROWS, 7 * ROWS)], load_sem.at[9])
    recent_copy.start()
    modes_copy = pltpu.make_async_copy(modes_in, modes, load_sem.at[10])
    modes_copy.start()

    z_hi, x_at, y_at = lax.div(gx, 16), lax.rem(lax.div(gx, 4), 4), lax.rem(gx, 4)
    z_lo, core_at = lax.div(gy, 2), lax.rem(gy, 2)
    z_part = [lax.rem(z_hi + 1 + j, 2) * 16 for j in range(2)]
    x_part = [lax.rem(x_at + 2 + j, 4) * 4 for j in range(4)]
    y_part = [lax.rem(y_at + 2 + j, 4) for j in range(4)]
    lo_part = [lax.rem(z_lo + j, 2) * 2 for j in range(2)]
    core_part = [lax.rem(core_at + j, 2) for j in range(2)]
    peers = []
    for jx in (0, 1, 3, 2):
        for jy in (0, 1, 3, 2):
            for jz in range(2):
                for jl in range(2):
                    for jc in range(2):
                        if (jx, jy, jz, jl, jc) != (2, 2, 1, 0, 0):
                            peers.append((z_part[jz] + x_part[jx] + y_part[jy], lo_part[jl] + core_part[jc]))

    barrier = pltpu.get_barrier_semaphore()
    for peer in peers:
        pl.semaphore_signal(barrier, inc=1, device_id=peer, device_id_type=MESH)

    solid_copy.wait()

    def collide(k, carry):
        x = lax.rem(k + 7, 8)
        plane_copy(x).wait()
        collide_plane(x, pops, solid, mo, nxt)
        return carry

    lax.fori_loop(0, 8, collide, 0)

    row_id = lax.broadcasted_iota(jnp.int32, (16, 128), 0)
    for piece in range(4):
        lanes = pl.ds(piece * 128, 128)
        inner, outer = plane_sums(nxt, 0, (2,), lanes)
        for slot, q in enumerate((0, 2, 3)):
            mxw[slot * 4 + piece] = inner[q] + jnp.where(row_id > 0, outer[q], 0.0)
            mxs[slot * 4 + piece] = mxw[slot * 4 + piece, pl.ds(0, 8, stride=2), :]
        mcs[piece, 0:1, :] = outer[0][0:1]
        mcs[piece, 1:2, :] = outer[3][0:1]
        for n, plane in enumerate((0, 2, 4, 6)):
            inner, outer = plane_sums(nxt, plane, (0, 1) if plane == 0 else (0, 1, 2), lanes)
            for q in range(4):
                sums[(n * 4 + q) * 4 + piece] = inner[q] + jnp.where(row_id > 0, outer[q], 0.0)
            for slot, q in enumerate((0, 1, 3)):
                r = n * 3 + slot
                mys[piece, r : r + 1, :] = outer[q][0:1]

    pl.semaphore_wait(barrier, NDEV - 1)

    def remote(src, dst, ssem, rsem, to):
        return pltpu.make_async_remote_copy(
            src_ref=src, dst_ref=dst, send_sem=ssem, recv_sem=rsem, device_id=to, device_id_type=MESH
        )

    heralds = [
        remote(mxs, mxr, small_ssem.at[0], small_rsem.at[0], (gx_up, gy)),
        remote(mcs, mcr, small_ssem.at[1], small_rsem.at[1], (gx_up, gy_up)),
        remote(mys, myr, small_ssem.at[2], small_rsem.at[2], (gx, gy_up)),
    ]
    for copy in heralds:
        copy.start()
    for copy in heralds:
        copy.wait_recv()

    first_row = lax.broadcasted_iota(jnp.int32, (8, 128), 0) == 0
    for piece in range(4):
        for n in range(4):
            dens, mx, my, mz = (
                sums[(n * 4 + q) * 4 + piece, pl.ds(0, 8, stride=2), :] for q in range(4)
            )
            rows = [jnp.where(first_row, myr[piece, n * 3 + s : n * 3 + s + 1, :], 0.0) for s in range(3)]
            dens, mx, my, mz = dens + rows[0], mx + rows[1], my + rows[0], mz + rows[2]
            if n == 0:
                part = [mxr[s * 4 + piece] for s in range(3)]
                edge = [jnp.where(first_row, mcr[piece, s : s + 1, :], 0.0) for s in range(2)]
                both = part[0] + edge[0]
                dens, mx, my, mz = dens + both, mx + both, my + part[1] + edge[0], mz + part[2] + edge[1]
            scale = vel_gain / dens
            field[piece, n * 32 : n * 32 + 8, :] = mx * scale
            field[piece, n * 32 + 8 : n * 32 + 16, :] = my * scale
            field[piece, n * 32 + 16 : n * 32 + 24, :] = mz * scale
            field[piece, n * 32 + 24 : n * 32 + 32, :] = jnp.zeros((8, 128), jnp.float32)
        turned[piece * 128 : (piece + 1) * 128, :] = jnp.transpose(field[piece])
    for b in range(2):
        parcel[pl.ds(b, NDEV, stride=2), :] = turned[pl.ds(2 * b, NDEV, stride=4), :]

    def to_all(source, target, index, rows):
        place = target.at[pl.ds(me * rows, rows)]
        for peer in peers:
            remote(source(peer), place, ex_ssem.at[index], ex_rsem.at[index], peer).start()
        pltpu.make_async_copy(source((gx, gy)), place, ex_rsem.at[index]).start()

    def all_here(target, index):
        pltpu.make_async_copy(target, target, ex_rsem.at[index]).wait()

    def all_sent(target, index, rows):
        part = target.at[pl.ds(0, (NDEV - 1) * rows)]
        pltpu.make_async_copy(part, part, ex_ssem.at[index]).wait()

    to_all(lambda peer: parcel.at[pl.ds(2 * (peer[0] * 4 + peer[1]), 2)], arrived, 0, 2)

    faces = [
        remote(nxt.at[2, :, :, 0], xr_up, bulk_ssem.at[0], bulk_rsem.at[0], (gx_up, gy)),
        remote(nxt.at[0, :, :, 7], xr_dn, bulk_ssem.at[1], bulk_rsem.at[1], (gx_dn, gy)),
        remote(nxt.at[:, 2, :, :, pl.ds(0, 1)], yr_up, bulk_ssem.at[2], bulk_rsem.at[2], (gx, gy_up)),
        remote(nxt.at[:, 0, :, :, pl.ds(15, 1)], yr_dn, bulk_ssem.at[3], bulk_rsem.at[3], (gx, gy_dn)),
        remote(nxt.at[2, 2, :, 0, pl.ds(0, 1)], corner.at[0], bulk_ssem.at[4], bulk_rsem.at[4], (gx_up, gy_up)),
        remote(nxt.at[2, 0, :, 0, pl.ds(15, 1)], corner.at[1], bulk_ssem.at[5], bulk_rsem.at[5], (gx_up, gy_dn)),
        remote(nxt.at[0, 2, :, 7, pl.ds(0, 1)], corner.at[2], bulk_ssem.at[6], bulk_rsem.at[6], (gx_dn, gy_up)),
        remote(nxt.at[0, 0, :, 7, pl.ds(15, 1)], corner.at[3], bulk_ssem.at[7], bulk_rsem.at[7], (gx_dn, gy_dn)),
    ]
    for copy in faces:
        copy.start()

    decay = [
        jnp.exp(jnp.full((8, 128), age_in[j], jnp.int32).astype(jnp.float32) * (-1.0 / age_span))
        for j in range(SNAPS)
    ]
    recent_copy.wait()
    for j in range(1, SNAPS):
        for k in range(24):
            at = pl.ds(j * ROWS + k * 8, 8)
            snaps[at, :] = snaps[at, :] * decay[j]
    modes_copy.wait()

    def project(block, carry):
        base = block * (4 * ROWS)
        acc = [[None] * 4 for _ in range(7)]
        for k in range(24):
            u = [modes[pl.ds(pl.multiple_of(base + n * ROWS + k * 8, 8), 8), :] for n in range(4)]
            for j in range(7):
                a = snaps[pl.ds((j + 1) * ROWS + k * 8, 8), :]
                for n in range(4):
                    term = a * u[n]
                    acc[j][n] = term if acc[j][n] is None else acc[j][n] + term
        for j in range(7):
            rows = [jnp.sum(acc[j][n], axis=0, keepdims=True) for n in range(4)]
            for n in range(4):
                stack[pl.ds((j + 1) * RANK + block * 4 + n, 1), :] = rows[n]
        return carry

    lax.fori_loop(0, RANK // 4, project, 0)
    ones = jnp.ones((8, 128), jnp.float32)

    def row_totals(block):
        return lax.dot_general(
            ones, block, (((1,), (1,)), ((), ())), precision=HIGHEST, preferred_element_type=jnp.float32
        )

    mine1[...] = jnp.zeros((8, 128), jnp.float32)
    for j in range(1, SNAPS):
        mine1[j : j + 1, 0:RANK] = row_totals(stack[j * RANK : (j + 1) * RANK, :])[0:1]
    to_all(lambda peer: mine1, got1, 1, 8)

    all_here(arrived, 0)
    lane = lax.broadcasted_iota(jnp.int32, (32, 128), 1)
    lane_block = lax.rem(lax.div(lane, 8), 4)
    for b in range(2):
        pieces = [arrived[pl.ds(2 * g + b, 32, stride=8), :] for g in range(4)]
        for c in range(3):
            out = None
            for g in range(4):
                moved = pieces[g] if g == c else pltpu.roll(pieces[g], ((g - c) * 8) % 128, 1)
                out = moved if out is None else jnp.where(lane_block == g, moved, out)
            snaps[pl.ds(c * 64 + b, 32, stride=2), :] = out
    fresh = [snaps[k * 8 : (k + 1) * 8, :] * decay[0] for k in range(24)]
    for k in range(24):
        snaps[k * 8 : (k + 1) * 8, :] = fresh[k]

    def project_fresh(block, carry):
        base = block * (8 * ROWS)
        for n in range(8):
            acc = None
            for k in range(24):
                at = pl.ds(pl.multiple_of(base + n * ROWS + k * 8, 8), 8)
                term = snaps[k * 8 : (k + 1) * 8, :] * modes[at, :]
                acc = term if acc is None else acc + term
            stack[pl.ds(block * 8 + n, 1), :] = jnp.sum(acc, axis=0, keepdims=True)
        return carry

    lax.fori_loop(0, RANK // 8, project_fresh, 0)
    mine2[...] = jnp.zeros((8, 128), jnp.float32)
    mine2[0:1, 0:RANK] = row_totals(stack[0:RANK, :])[0:1]
    to_all(lambda peer: mine2.at[pl.ds(0, 1)], got2, 2, 1)

    for copy in heralds:
        copy.wait_send()
    for copy in faces:
        copy.wait()
    fixes = [
        [
            pltpu.make_async_copy(xr_up, nxt.at[2, :, :, 0], fix_sem.at[0]),
            pltpu.make_async_copy(xr_dn, nxt.at[0, :, :, 7], fix_sem.at[1]),
        ],
        [
            pltpu.make_async_copy(yr_up, nxt.at[:, 2, :, :, pl.ds(0, 1)], fix_sem.at[2]),
            pltpu.make_async_copy(yr_dn, nxt.at[:, 0, :, :, pl.ds(15, 1)], fix_sem.at[3]),
        ],
        [
            pltpu.make_async_copy(corner.at[0], nxt.at[2, 2, :, 0, pl.ds(0, 1)], fix_sem.at[4]),
            pltpu.make_async_copy(corner.at[1], nxt.at[2, 0, :, 0, pl.ds(15, 1)], fix_sem.at[5]),
            pltpu.make_async_copy(corner.at[2], nxt.at[0, 2, :, 7, pl.ds(0, 1)], fix_sem.at[6]),
            pltpu.make_async_copy(corner.at[3], nxt.at[0, 0, :, 7, pl.ds(15, 1)], fix_sem.at[7]),
        ],
    ]
    for copy in fixes[0]:
        copy.start()

    all_here(got1, 1)
    total = got1[0:8, :]
    for d in range(1, NDEV):
        total = total + got1[d * 8 : (d + 1) * 8, :]
    total = total * (1.0 / TOTAL)
    small[0:8, :] = total

    def spread_row(j, row):
        spread[j * 128 : (j + 1) * 128, :] = jnp.transpose(jnp.broadcast_to(row, (128, 128)))

    for j in range(1, SNAPS):
        spread_row(j, total[j : j + 1])

    def subtract(k, carry):
        base = k * 32
        acc = [
            [snaps[pl.ds(pl.multiple_of(base + j * ROWS + n * 8, 8), 8), :] for n in range(4)]
            for j in range(1, SNAPS)
        ]

        for m in range(RANK):
            u = [modes[pl.ds(pl.multiple_of(base + m * ROWS + n * 8, 8), 8), :] for n in range(4)]
            for j in range(7):
                c = spread[(j + 1) * 128 + m : (j + 1) * 128 + m + 1, :]
                for n in range(4):
                    acc[j][n] = acc[j][n] - c * u[n]
        for j in range(7):
            for n in range(4):
                resid[pl.ds(pl.multiple_of(base + (j + 1) * ROWS + n * 8, 8), 8), :] = acc[j][n]
        return carry

    lax.fori_loop(0, ROWS // 32, subtract, 0)

    def inner_product(i, j):
        acc = None
        for k in range(24):
            term = resid[i * ROWS + k * 8 : i * ROWS + k * 8 + 8, :] * resid[j * ROWS + k * 8 : j * ROWS + k * 8 + 8, :]
            acc = term if acc is None else acc + term
        return jnp.sum(acc, axis=0, keepdims=True)

    stack[0 : 2 * RANK, :] = jnp.zeros((2 * RANK, 128), jnp.float32)
    for i in range(1, SNAPS):
        for j in range(1, i + 1):
            stack[i * 8 + j : i * 8 + j + 1, :] = inner_product(i, j)

    for copy in fixes[0]:
        copy.wait()
    for copy in fixes[1]:
        copy.start()
    for copy in fixes[1]:
        copy.wait()
    for copy in fixes[2]:
        copy.start()

    all_here(got2, 2)
    row = jnp.sum(got2[...], axis=0, keepdims=True) * (1.0 / TOTAL)
    small[0:1, :] = row
    spread_row(0, row)

    def subtract_fresh(k, carry):
        base = k * 64
        acc = [snaps[pl.ds(pl.multiple_of(base + n * 8, 8), 8), :] for n in range(8)]
        for m in range(RANK):
            c = spread[m : m + 1, :]
            for n in range(8):
                acc[n] = acc[n] - c * modes[pl.ds(pl.multiple_of(base + m * ROWS + n * 8, 8), 8), :]
        for n in range(8):
            resid[pl.ds(pl.multiple_of(base + n * 8, 8), 8), :] = acc[n]
        return carry

    lax.fori_loop(0, ROWS // 64, subtract_fresh, 0)
    for i in range(SNAPS):
        stack[i * 8 : i * 8 + 1, :] = inner_product(i, 0)
    mine3[...] = jnp.zeros((8, 128), jnp.float32)
    mine3[0:1, :] = row_totals(stack[0:128, :])[0:1]
    to_all(lambda peer: mine3.at[pl.ds(0, 1)], got3, 3, 1)
    for copy in fixes[2]:
        copy.wait()
    all_sent(arrived, 0, 2)
    all_sent(got1, 1, 8)
    all_sent(got2, 2, 1)
    all_here(got3, 3)
    small[8:16, :] = jnp.broadcast_to(jnp.sum(got3[...], axis=0, keepdims=True) * (1.0 / TOTAL), (8, 128))
    all_sent(got3, 3, 1)


def last_kernel(nxt, resid, small, singular, nxt_out, dirs_out, core_out, dirs, gram, wide, sem):
    bulk = pltpu.make_async_copy(nxt, nxt_out, sem.at[0])
    bulk.start()
    gram[...] = jnp.transpose(jnp.broadcast_to(small[8:9, :], (128, 128)))
    low = [[None] * SNAPS for _ in range(SNAPS)]
    inv_diag = [None] * SNAPS
    for j in range(SNAPS):
        diag = gram[j * 8 + j : j * 8 + j + 1, :]
        for k in range(j):
            diag = diag - low[j][k] * low[j][k]
        low[j][j] = jnp.sqrt(diag)
        inv_diag[j] = 1.0 / low[j][j]
        for i in range(j + 1, SNAPS):
            value = gram[i * 8 + j : i * 8 + j + 1, :]
            for k in range(j):
                value = value - low[i][k] * low[j][k]
            low[i][j] = value * inv_diag[j]
    inverse = [[None] * SNAPS for _ in range(SNAPS)]
    for j in range(SNAPS):
        inverse[j][j] = inv_diag[j]
        for i in range(j + 1, SNAPS):
            value = None
            for k in range(j, i):
                term = low[i][k] * inverse[k][j]
                value = term if value is None else value + term
            inverse[i][j] = -value * inv_diag[i]
    for i in range(SNAPS):
        factors = [jnp.broadcast_to(inverse[i][j], (8, 128)) for j in range(i + 1)]
        for k in range(24):
            acc = None
            for j in range(i + 1):
                term = factors[j] * resid[j * ROWS + k * 8 : j * ROWS + k * 8 + 8, :]
                acc = term if acc is None else acc + term
            dirs[i * ROWS + k * 8 : i * ROWS + k * 8 + 8, :] = acc
    out = pltpu.make_async_copy(dirs, dirs_out, sem.at[1])
    out.start()

    row_id = lax.broadcasted_iota(jnp.int32, (RANK, 128), 0)
    lane_id = lax.broadcasted_iota(jnp.int32, (RANK, 128), 1)
    wide[...] = jnp.zeros((128, 128), jnp.float32)
    wide[127:128, 0:RANK] = singular[...]
    wide[0:RANK, :] = jnp.where(row_id == lane_id, jnp.broadcast_to(wide[127:128, :], (RANK, 128)), 0.0)
    row8 = lax.broadcasted_iota(jnp.int32, (8, 128), 0)
    lane8 = lax.broadcasted_iota(jnp.int32, (8, 128), 1)
    block = jnp.where(lane8 < RANK, small[0:8, :], 0.0)
    for i in range(SNAPS):
        for j in range(i + 1):
            block = jnp.where((row8 == i) & (lane8 == RANK + j), low[i][j], block)
    wide[RANK : RANK + 8, :] = block
    core_out[...] = jnp.transpose(wide[...])[0 : RANK + 8, 0 : RANK + 8]
    bulk.wait()
    out.wait()


def per_device(populations, solid, basis, singular, recent, age):
    f32 = jnp.float32
    vmem, hbm, smem = pltpu.VMEM, pltpu.HBM, pltpu.SMEM
    modes = basis.reshape(RANK, 3, 2, 32, 128).transpose(0, 1, 3, 2, 4).reshape(RANK * ROWS, 128)
    earlier = recent.reshape(7, 3, 2, 32, 128).transpose(0, 1, 3, 2, 4).reshape(7 * ROWS, 128)
    dma = pltpu.SemaphoreType.DMA
    in_hbm = pl.BlockSpec(memory_space=hbm)
    in_vmem = pl.BlockSpec(memory_space=vmem)
    nxt, resid, small = pl.pallas_call(
        main_kernel,
        out_shape=(
            vmem((3, 3, 3, 8, 16, 512), f32),
            vmem((SNAPS * ROWS, 128), f32),
            vmem((16, 128), f32),
        ),
        in_specs=[in_hbm, in_hbm, in_hbm, in_hbm, pl.BlockSpec(memory_space=smem)],
        out_specs=(in_vmem, in_vmem, in_vmem),
        scratch_shapes=[
            vmem((27, 8, 16, 512), f32),
            vmem((8, 16, 512), jnp.int32),
            vmem((RANK * ROWS, 128), f32),
            vmem((SNAPS * ROWS, 128), f32),
            vmem((5, 16, 512), f32),
            vmem((64, 16, 128), f32),
            vmem((12, 16, 128), f32),
            vmem((12, 8, 128), f32),
            vmem((12, 8, 128), f32),
            vmem((4, 16, 128), f32),
            vmem((4, 16, 128), f32),
            vmem((4, 8, 128), f32),
            vmem((4, 8, 128), f32),
            vmem((4, 128, 128), f32),
            vmem((512, 128), f32),
            vmem((2 * NDEV, 128), f32),
            vmem((2 * NDEV, 128), f32),
            vmem((3, 3, 16, 512), f32),
            vmem((3, 3, 16, 512), f32),
            vmem((3, 3, 8, 1, 512), f32),
            vmem((3, 3, 8, 1, 512), f32),
            vmem((4, 3, 1, 512), f32),
            vmem((SNAPS * RANK, 128), f32),
            vmem((8, 128), f32),
            vmem((NDEV * 8, 128), f32),
            vmem((8, 128), f32),
            vmem((NDEV, 128), f32),
            vmem((8, 128), f32),
            vmem((NDEV, 128), f32),
            vmem((SNAPS * 128, 128), f32),
            dma((11,)),
            dma((3,)),
            dma((3,)),
            dma((8,)),
            dma((8,)),
            dma((4,)),
            dma((4,)),
            dma((8,)),
        ],
        compiler_params=pltpu.CompilerParams(
            collective_id=0, has_side_effects=True, vmem_limit_bytes=40 * 2**20
        ),
    )(populations, solid, modes, earlier, age)
    nxt_out, dirs, core = pl.pallas_call(
        last_kernel,
        out_shape=(
            jax.ShapeDtypeStruct((3, 3, 3, 8, 16, 512), f32),
            jax.ShapeDtypeStruct((SNAPS * ROWS, 128), f32),
            jax.ShapeDtypeStruct((RANK + 8, RANK + 8), f32),
        ),
        in_specs=[in_vmem, in_vmem, in_vmem, in_vmem],
        out_specs=(in_hbm, in_hbm, in_vmem),
        scratch_shapes=[vmem((SNAPS * ROWS, 128), f32), vmem((128, 128), f32), vmem((128, 128), f32), dma((2,))],
        compiler_params=pltpu.CompilerParams(vmem_limit_bytes=24 * 2**20),
    )(nxt, resid, small, singular.reshape(1, RANK))
    directions = dirs.reshape(SNAPS, 3, 32, 2, 128).transpose(0, 1, 3, 2, 4).reshape(SNAPS, 3, 2, 4096)
    return nxt_out.reshape(27, 8, 16, 512), directions, core


def solution(mesh):
    return jax.shard_map(
        per_device,
        mesh=mesh,
        in_specs=(
            P(None, "gx", "gy", None),
            P("gx", "gy", None),
            P(None, None, ("gx", "gy"), None),
            P(),
            P(None, None, ("gx", "gy"), None),
            P(),
        ),
        out_specs=(P(None, "gx", "gy", None), P(None, None, ("gx", "gy"), None), P()),
        check_vma=False,
    )
```

profile of v0, /device:TPU:1, one launch (start us, length us, event | category | flops | bytes accessed | tf_op | source)
XLA Modules:
  0.0 55.4 jit_solution(1490040317551567697)
XLA Ops:
  0.6 0.0 copy-start
  0.6 1.1 %copy-done = f32[7,3,2,4096]{3,2,1,0:T(2,128)S(1)} copy-done((f32[7,3,2,4096]{3,2,1,0:T(2,128)S(1)}, f32[7,3,2,4096]{3,2,1,0:T(2,128)}, u32[]{:S(2)}) %copy-start) | copy-done | bytes 688152
  1.7 0.0 copy-start.1
  1.7 0.9 %copy-done.1 = s32[8,16,512]{2,1,0:T(8,128)S(1)} copy-done((s32[8,16,512]{2,1,0:T(8,128)S(1)}, s32[8,16,512]{2,1,0:T(8,128)}, u32[]{:S(2)}) %copy-start.1) | copy-done | bytes 262168
  2.7 0.0 copy-start.2
  2.7 0.7 %copy-done.2 = s32[8]{0:T(128)S(1)} copy-done((s32[8]{0:T(128)S(1)}, s32[8]{0:T(128)}, u32[]{:S(2)}) %copy-start.2) | copy-done | bytes 56
  3.3 0.0 copy-start.3
  3.3 47.9 %shard_map.85 = (f32[3,3,3,8,16,512]{5,4,3,2,1,0:T(8,128)S(1)}, f32[1536,128]{1,0:T(8,128)S(1)}, f32[16,128]{1,0:T(8,128)S(1)}) custom-call(f32[27,8,16,512]{3,2,1,0:T(8,128)} %pops_in.1, s32[8,16,512]{2,1,0:T(8,128)S(1)} %copy-done.1, f32[12288,128]{1,0:T(8,128)} %bitcast.19, f32[1344,128]{1,0:T(8,128)S(1)} %bitcast.17, s32[8]{0:T(128)S(1)} %copy-done.2), custom_call_target="tpu_custom_call" | custom-call | tf_op jit(solution)/shard_map/pallas_call | solution.py:493
  51.3 0.0 copy-done.3
  51.3 4.1 %shard_map.86 = (f32[3,3,3,8,16,512]{5,4,3,2,1,0:T(8,128)}, f32[1536,128]{1,0:T(8,128)}, f32[72,72]{1,0:T(8,128)}) custom-call(f32[3,3,3,8,16,512]{5,4,3,2,1,0:T(8,128)S(1)} %get-tuple-element.9.nxt, f32[1536,128]{1,0:T(8,128)S(1)} %get-tuple-element.10.resid, f32[16,128]{1,0:T(8,128)S(1)} %get-tuple-element.11.small, f32[1,64]{1,0:T(1,128)S(1)} %bitcast.18), custom_call_target="tpu_custom_call" | custom-call | tf_op jit(solution)/shard_map/pallas_call | solution.py:546
Async XLA Ops:
  0.6 1.1 %copy-start = (f32[7,3,2,4096]{3,2,1,0:T(2,128)S(1)}, f32[7,3,2,4096]{3,2,1,0:T(2,128)}, u32[]{:S(2)}) copy-start(f32[7,3,2,4096]{3,2,1,0:T(2,128)} %param.10) | copy-start | bytes 2064388
  1.7 0.9 %copy-start.1 = (s32[8,16,512]{2,1,0:T(8,128)S(1)}, s32[8,16,512]{2,1,0:T(8,128)}, u32[]{:S(2)}) copy-start(s32[8,16,512]{2,1,0:T(8,128)} %solid_in.1) | copy-start | bytes 786436
  2.7 0.7 %copy-start.2 = (s32[8]{0:T(128)S(1)}, s32[8]{0:T(128)}, u32[]{:S(2)}) copy-start(s32[8]{0:T(128)} %age_in.1) | copy-start | bytes 100
  3.3 47.9 %copy-start.3 = (f32[64]{0:T(128)S(1)}, f32[64]{0:T(128)}, u32[]{:S(2)}) copy-start(f32[64]{0:T(128)} %param.9) | copy-start | bytes 772
where the time goes:
time: 55.6 us; the launch traced here: 55.4 us
  Pallas kernels  52.1 us (94%)
  local copies, waits for them, and re-layouts  2.7 us (5%)
  between operations  0.66 us (1%)
    pallas_call x1, Pallas kernels, per_device(): pl.pallas_call(main_kernel, out_shape=(vmem((3, 3, 3, 8, 16, 512), f32),...  47.9 us
    pallas_call x1, Pallas kernels, per_device(): pl.pallas_call(last_kernel, out_shape=(jax.ShapeDtypeStruct((3, 3, 3, 8,...  4.14 us
    unnamed x8, local copies, waits for them, and re-layouts  2.7 us

commit v1 on v0

--- a/solution.py
+++ b/solution.py
@@ -111,10 +111,9 @@
 def main_kernel(
     pops_in, solid_in, modes_in, recent_in, age_in,
     nxt, resid, small,
-    pops, solid, modes, snaps, mo, sums, mxw, mxs, mxr, mys, myr, mcs, mcr,
-    field, turned, parcel, arrived, xr_up, xr_dn, yr_up, yr_dn, corner,
+    pops, solid, modes, snaps, mo, sums, field, beyond, turned, parcel, arrived, xr_up, xr_dn, yr_up, yr_dn, corner,
     stack, mine1, got1, mine2, got2, mine3, got3, spread,
-    load_sem, small_ssem, small_rsem, bulk_ssem, bulk_rsem, ex_ssem, ex_rsem, fix_sem,
+    age, load_sem, bulk_ssem, bulk_rsem, ex_ssem, ex_rsem, fix_sem,
 ):
     gx, gy = lax.axis_index("gx"), lax.axis_index("gy")
     me = gx * 4 + gy
@@ -133,6 +132,8 @@
     recent_copy.start()
     modes_copy = pltpu.make_async_copy(modes_in, modes, load_sem.at[10])
     modes_copy.start()
+    age_copy = pltpu.make_async_copy(age_in, age, load_sem.at[11])
+    age_copy.start()
 
     z_hi, x_at, y_at = lax.div(gx, 16), lax.rem(lax.div(gx, 4), 4), lax.rem(gx, 4)
     z_lo, core_at = lax.div(gy, 2), lax.rem(gy, 2)
@@ -165,21 +166,40 @@
     lax.fori_loop(0, 8, collide, 0)
 
     row_id = lax.broadcasted_iota(jnp.int32, (16, 128), 0)
+    first_row = lax.broadcasted_iota(jnp.int32, (8, 128), 0) == 0
+    second_row = lax.broadcasted_iota(jnp.int32, (8, 128), 0) == 1
+
+    def edge_rows(outer):
+        return [jnp.broadcast_to(value[0:1], (8, 128)) for value in outer]
+
     for piece in range(4):
         lanes = pl.ds(piece * 128, 128)
         inner, outer = plane_sums(nxt, 0, (2,), lanes)
-        for slot, q in enumerate((0, 2, 3)):
-            mxw[slot * 4 + piece] = inner[q] + jnp.where(row_id > 0, outer[q], 0.0)
-            mxs[slot * 4 + piece] = mxw[slot * 4 + piece, pl.ds(0, 8, stride=2), :]
-        mcs[piece, 0:1, :] = outer[0][0:1]
-        mcs[piece, 1:2, :] = outer[3][0:1]
+        diagonal = edge_rows(outer)
+        for q in range(4):
+            sums[piece, 16 + q] = inner[q] + jnp.where(row_id > 0, outer[q], 0.0)
+        along_y = []
         for n, plane in enumerate((0, 2, 4, 6)):
             inner, outer = plane_sums(nxt, plane, (0, 1) if plane == 0 else (0, 1, 2), lanes)
+            along_y.append(edge_rows(outer))
             for q in range(4):
-                sums[(n * 4 + q) * 4 + piece] = inner[q] + jnp.where(row_id > 0, outer[q], 0.0)
-            for slot, q in enumerate((0, 1, 3)):
-                r = n * 3 + slot
-                mys[piece, r : r + 1, :] = outer[q][0:1]
+                sums[piece, n * 4 + q] = inner[q] + jnp.where(row_id > 0, outer[q], 0.0)
+        for q in range(4):
+            for n in range(4):
+                at = pl.ds(n * 32 + q * 8, 8)
+                field[piece, at, :] = sums[piece, n * 4 + q, pl.ds(0, 8, stride=2), :]
+                if n == 0:
+                    beyond[piece, at, :] = sums[piece, 16 + q, pl.ds(0, 8, stride=2), :]
+                else:
+                    second = (None, along_y[0][q], diagonal[q], 0.0)[n]
+                    beyond[piece, at, :] = jnp.where(
+                        first_row, along_y[n][q], jnp.where(second_row, second, 0.0)
+                    )
+        turned[0, piece * 128 : (piece + 1) * 128, :] = jnp.transpose(field[piece])
+        turned[1, piece * 128 : (piece + 1) * 128, :] = jnp.transpose(beyond[piece])
+    for f in range(2):
+        for b in range(2):
+            parcel[pl.ds(2 * f + b, NDEV, stride=4), :] = turned[f, pl.ds(2 * b, NDEV, stride=4), :]
 
     pl.semaphore_wait(barrier, NDEV - 1)
 
@@ -187,53 +207,6 @@
         return pltpu.make_async_remote_copy(
             src_ref=src, dst_ref=dst, send_sem=ssem, recv_sem=rsem, device_id=to, device_id_type=MESH
         )
-
-    heralds = [
-        remote(mxs, mxr, small_ssem.at[0], small_rsem.at[0], (gx_up, gy)),
-        remote(mcs, mcr, small_ssem.at[1], small_rsem.at[1], (gx_up, gy_up)),
-        remote(mys, myr, small_ssem.at[2], small_rsem.at[2], (gx, gy_up)),
-    ]
-    for copy in heralds:
-        copy.start()
-    for copy in heralds:
-        copy.wait_recv()
-
-    first_row = lax.broadcasted_iota(jnp.int32, (8, 128), 0) == 0
-    for piece in range(4):
-        for n in range(4):
-            dens, mx, my, mz = (
-                sums[(n * 4 + q) * 4 + piece, pl.ds(0, 8, stride=2), :] for q in range(4)
-            )
-            rows = [jnp.where(first_row, myr[piece, n * 3 + s : n * 3 + s + 1, :], 0.0) for s in range(3)]
-            dens, mx, my, mz = dens + rows[0], mx + rows[1], my + rows[0], mz + rows[2]
-            if n == 0:
-                part = [mxr[s * 4 + piece] for s in range(3)]
-                edge = [jnp.where(first_row, mcr[piece, s : s + 1, :], 0.0) for s in range(2)]
-                both = part[0] + edge[0]
-                dens, mx, my, mz = dens + both, mx + both, my + part[1] + edge[0], mz + part[2] + edge[1]
-            scale = vel_gain / dens
-            field[piece, n * 32 : n * 32 + 8, :] = mx * scale
-            field[piece, n * 32 + 8 : n * 32 + 16, :] = my * scale
-            field[piece, n * 32 + 16 : n * 32 + 24, :] = mz * scale
-            field[piece, n * 32 + 24 : n * 32 + 32, :] = jnp.zeros((8, 128), jnp.float32)
-        turned[piece * 128 : (piece + 1) * 128, :] = jnp.transpose(field[piece])
-    for b in range(2):
-        parcel[pl.ds(b, NDEV, stride=2), :] = turned[pl.ds(2 * b, NDEV, stride=4), :]
-
-    def to_all(source, target, index, rows):
-        place = target.at[pl.ds(me * rows, rows)]
-        for peer in peers:
-            remote(source(peer), place, ex_ssem.at[index], ex_rsem.at[index], peer).start()
-        pltpu.make_async_copy(source((gx, gy)), place, ex_rsem.at[index]).start()
-
-    def all_here(target, index):
-        pltpu.make_async_copy(target, target, ex_rsem.at[index]).wait()
-
-    def all_sent(target, index, rows):
-        part = target.at[pl.ds(0, (NDEV - 1) * rows)]
-        pltpu.make_async_copy(part, part, ex_ssem.at[index]).wait()
-
-    to_all(lambda peer: parcel.at[pl.ds(2 * (peer[0] * 4 + peer[1]), 2)], arrived, 0, 2)
 
     faces = [
         remote(nxt.at[2, :, :, 0], xr_up, bulk_ssem.at[0], bulk_rsem.at[0], (gx_up, gy)),
@@ -245,11 +218,24 @@
         remote(nxt.at[0, 2, :, 7, pl.ds(0, 1)], corner.at[2], bulk_ssem.at[6], bulk_rsem.at[6], (gx_dn, gy_up)),
         remote(nxt.at[0, 0, :, 7, pl.ds(15, 1)], corner.at[3], bulk_ssem.at[7], bulk_rsem.at[7], (gx_dn, gy_dn)),
     ]
-    for copy in faces:
-        copy.start()
-
+    def to_all(source, target, index, rows):
+        place = target.at[pl.ds(me * rows, rows)]
+        for peer in peers:
+            remote(source(peer), place, ex_ssem.at[index], ex_rsem.at[index], peer).start()
+        pltpu.make_async_copy(source((gx, gy)), place, ex_rsem.at[index]).start()
+
+    def all_here(target, index):
+        pltpu.make_async_copy(target, target, ex_rsem.at[index]).wait()
+
+    def all_sent(target, index, rows):
+        part = target.at[pl.ds(0, (NDEV - 1) * rows)]
+        pltpu.make_async_copy(part, part, ex_ssem.at[index]).wait()
+
+    to_all(lambda peer: parcel.at[pl.ds(4 * (peer[0] * 4 + peer[1]), 4)], arrived, 0, 4)
+
+    age_copy.wait()
     decay = [
-        jnp.exp(jnp.full((8, 128), age_in[j], jnp.int32).astype(jnp.float32) * (-1.0 / age_span))
+        jnp.exp(jnp.full((8, 128), age[j], jnp.int32).astype(jnp.float32) * (-1.0 / age_span))
         for j in range(SNAPS)
     ]
     recent_copy.wait()
@@ -283,22 +269,47 @@
             ones, block, (((1,), (1,)), ((), ())), precision=HIGHEST, preferred_element_type=jnp.float32
         )
 
-    mine1[...] = jnp.zeros((8, 128), jnp.float32)
-    for j in range(1, SNAPS):
-        mine1[j : j + 1, 0:RANK] = row_totals(stack[j * RANK : (j + 1) * RANK, :])[0:1]
-    to_all(lambda peer: mine1, got1, 1, 8)
+    stack[0:RANK, :] = jnp.zeros((RANK, 128), jnp.float32)
+    for r in range(4):
+        mine1[r : r + 1, :] = row_totals(stack[r * 128 : (r + 1) * 128, :])[0:1]
+
+
+    to_all(lambda peer: mine1.at[pl.ds(0, 4)], got1, 1, 4)
 
     all_here(arrived, 0)
     lane = lax.broadcasted_iota(jnp.int32, (32, 128), 1)
     lane_block = lax.rem(lax.div(lane, 8), 4)
+    in_x, in_y = lax.div(lane, 32), lax.rem(lane, 8)
+
+    def lane_roll(value, by):
+        by = by % 128
+        return pltpu.roll(value, by, 1) if by else value
+
+    def from_before(value):
+        return pltpu.roll(value, 1, 0)
+
+    def pick(values):
+        out = values[0]
+        for g in range(1, 4):
+            out = jnp.where(lane_block == g, values[g], out)
+        return out
+
     for b in range(2):
-        pieces = [arrived[pl.ds(2 * g + b, 32, stride=8), :] for g in range(4)]
+        own = [arrived[pl.ds(4 * g + b, 32, stride=16), :] for g in range(4)]
+        other = [arrived[pl.ds(4 * g + 2 + b, 32, stride=16), :] for g in range(4)]
+        whole = []
+        for g in range(4):
+            below = other[(g + 3) % 4]
+            corners = lane_roll(below, -33) + from_before(lane_roll(below, -65))
+            whole.append(
+                own[g]
+                + jnp.where(in_x == 0, from_before(other[g]), jnp.where(in_y == 0, below, 0.0))
+                + jnp.where((in_x == 0) & (in_y == 0), corners, 0.0)
+            )
+        scale = vel_gain / pick([lane_roll(whole[g], g * 8) for g in range(4)])
         for c in range(3):
-            out = None
-            for g in range(4):
-                moved = pieces[g] if g == c else pltpu.roll(pieces[g], ((g - c) * 8) % 128, 1)
-                out = moved if out is None else jnp.where(lane_block == g, moved, out)
-            snaps[pl.ds(c * 64 + b, 32, stride=2), :] = out
+            moved = pick([lane_roll(whole[g], (g - c - 1) * 8) for g in range(4)])
+            snaps[pl.ds(c * 64 + b, 32, stride=2), :] = moved * scale
     fresh = [snaps[k * 8 : (k + 1) * 8, :] * decay[0] for k in range(24)]
     for k in range(24):
         snaps[k * 8 : (k + 1) * 8, :] = fresh[k]
@@ -319,8 +330,80 @@
     mine2[0:1, 0:RANK] = row_totals(stack[0:RANK, :])[0:1]
     to_all(lambda peer: mine2.at[pl.ds(0, 1)], got2, 2, 1)
 
-    for copy in heralds:
-        copy.wait_send()
+    for copy in faces:
+        copy.start()
+
+    all_here(got1, 1)
+    total = got1[0:8, :]
+    for d in range(1, NDEV // 2):
+        total = total + got1[d * 8 : (d + 1) * 8, :]
+    total = (total[0:4] + total[4:8]) * (1.0 / TOTAL)
+
+    def spread_row(r, row):
+        spread[r * 128 : (r + 1) * 128, :] = jnp.transpose(jnp.broadcast_to(row, (128, 128)))
+
+    for r in range(4):
+        spread_row(r, total[r : r + 1])
+    for j in range(1, SNAPS):
+        small[j : j + 1, 0:RANK] = total[j // 2 : j // 2 + 1, (j % 2) * RANK : (j % 2 + 1) * RANK]
+
+    def subtract(k, carry):
+        base = k * 32
+        acc = [
+            [snaps[pl.ds(pl.multiple_of(base + j * ROWS + n * 8, 8), 8), :] for n in range(4)]
+            for j in range(1, SNAPS)
+        ]
+
+        for m in range(RANK):
+            u = [modes[pl.ds(pl.multiple_of(base + m * ROWS + n * 8, 8), 8), :] for n in range(4)]
+            for j in range(7):
+                c = spread[(j + 1) * RANK + m : (j + 1) * RANK + m + 1, :]
+                for n in range(4):
+                    acc[j][n] = acc[j][n] - c * u[n]
+        for j in range(7):
+            for n in range(4):
+                resid[pl.ds(pl.multiple_of(base + (j + 1) * ROWS + n * 8, 8), 8), :] = acc[j][n]
+        return carry
+
+    lax.fori_loop(0, ROWS // 32, subtract, 0)
+
+    def inner_products(pairs):
+        acc = {}
+        for k in range(24):
+            r = {}
+            for pair in pairs:
+                for i in pair:
+                    if i not in r:
+                        r[i] = resid[i * ROWS + k * 8 : i * ROWS + k * 8 + 8, :]
+                term = r[pair[0]] * r[pair[1]]
+                acc[pair] = acc[pair] + term if pair in acc else term
+        for i, j in pairs:
+            stack[i * 8 + j : i * 8 + j + 1, :] = jnp.sum(acc[i, j], axis=0, keepdims=True)
+
+    stack[0:128, :] = jnp.zeros((128, 128), jnp.float32)
+    inner_products([(i, j) for i in range(1, SNAPS) for j in range(1, i + 1)])
+
+    all_here(got2, 2)
+    row = jnp.sum(got2[...], axis=0, keepdims=True) * (1.0 / TOTAL)
+    small[0:1, :] = row
+    spread_row(4, row)
+
+    def subtract_fresh(k, carry):
+        base = k * 64
+        acc = [snaps[pl.ds(pl.multiple_of(base + n * 8, 8), 8), :] for n in range(8)]
+        for m in range(RANK):
+            c = spread[4 * 128 + m : 4 * 128 + m + 1, :]
+            for n in range(8):
+                acc[n] = acc[n] - c * modes[pl.ds(pl.multiple_of(base + m * ROWS + n * 8, 8), 8), :]
+        for n in range(8):
+            resid[pl.ds(pl.multiple_of(base + n * 8, 8), 8), :] = acc[n]
+        return carry
+
+    lax.fori_loop(0, ROWS // 64, subtract_fresh, 0)
+    inner_products([(i, 0) for i in range(SNAPS)])
+    mine3[...] = jnp.zeros((8, 128), jnp.float32)
+    mine3[0:1, :] = row_totals(stack[0:128, :])[0:1]
+    to_all(lambda peer: mine3.at[pl.ds(0, 1)], got3, 3, 1)
     for copy in faces:
         copy.wait()
     fixes = [
@@ -342,51 +425,6 @@
     for copy in fixes[0]:
         copy.start()
 
-    all_here(got1, 1)
-    total = got1[0:8, :]
-    for d in range(1, NDEV):
-        total = total + got1[d * 8 : (d + 1) * 8, :]
-    total = total * (1.0 / TOTAL)
-    small[0:8, :] = total
-
-    def spread_row(j, row):
-        spread[j * 128 : (j + 1) * 128, :] = jnp.transpose(jnp.broadcast_to(row, (128, 128)))
-
-    for j in range(1, SNAPS):
-        spread_row(j, total[j : j + 1])
-
-    def subtract(k, carry):
-        base = k * 32
-        acc = [
-            [snaps[pl.ds(pl.multiple_of(base + j * ROWS + n * 8, 8), 8), :] for n in range(4)]
-            for j in range(1, SNAPS)
-        ]
-
-        for m in range(RANK):
-            u = [modes[pl.ds(pl.multiple_of(base + m * ROWS + n * 8, 8), 8), :] for n in range(4)]
-            for j in range(7):
-                c = spread[(j + 1) * 128 + m : (j + 1) * 128 + m + 1, :]
-                for n in range(4):
-                    acc[j][n] = acc[j][n] - c * u[n]
-        for j in range(7):
-            for n in range(4):
-                resid[pl.ds(pl.multiple_of(base + (j + 1) * ROWS + n * 8, 8), 8), :] = acc[j][n]
-        return carry
-
-    lax.fori_loop(0, ROWS // 32, subtract, 0)
-
-    def inner_product(i, j):
-        acc = None
-        for k in range(24):
-            term = resid[i * ROWS + k * 8 : i * ROWS + k * 8 + 8, :] * resid[j * ROWS + k * 8 : j * ROWS + k * 8 + 8, :]
-            acc = term if acc is None else acc + term
-        return jnp.sum(acc, axis=0, keepdims=True)
-
-    stack[0 : 2 * RANK, :] = jnp.zeros((2 * RANK, 128), jnp.float32)
-    for i in range(1, SNAPS):
-        for j in range(1, i + 1):
-            stack[i * 8 + j : i * 8 + j + 1, :] = inner_product(i, j)
-
     for copy in fixes[0]:
         copy.wait()
     for copy in fixes[1]:
@@ -396,32 +434,10 @@
     for copy in fixes[2]:
         copy.start()
 
-    all_here(got2, 2)
-    row = jnp.sum(got2[...], axis=0, keepdims=True) * (1.0 / TOTAL)
-    small[0:1, :] = row
-    spread_row(0, row)
-
-    def subtract_fresh(k, carry):
-        base = k * 64
-        acc = [snaps[pl.ds(pl.multiple_of(base + n * 8, 8), 8), :] for n in range(8)]
-        for m in range(RANK):
-            c = spread[m : m + 1, :]
-            for n in range(8):
-                acc[n] = acc[n] - c * modes[pl.ds(pl.multiple_of(base + m * ROWS + n * 8, 8), 8), :]
-        for n in range(8):
-            resid[pl.ds(pl.multiple_of(base + n * 8, 8), 8), :] = acc[n]
-        return carry
-
-    lax.fori_loop(0, ROWS // 64, subtract_fresh, 0)
-    for i in range(SNAPS):
-        stack[i * 8 : i * 8 + 1, :] = inner_product(i, 0)
-    mine3[...] = jnp.zeros((8, 128), jnp.float32)
-    mine3[0:1, :] = row_totals(stack[0:128, :])[0:1]
-    to_all(lambda peer: mine3.at[pl.ds(0, 1)], got3, 3, 1)
     for copy in fixes[2]:
         copy.wait()
-    all_sent(arrived, 0, 2)
-    all_sent(got1, 1, 8)
+    all_sent(arrived, 0, 4)
+    all_sent(got1, 1, 4)
     all_sent(got2, 2, 1)
     all_here(got3, 3)
     small[8:16, :] = jnp.broadcast_to(jnp.sum(got3[...], axis=0, keepdims=True) * (1.0 / TOTAL), (8, 128))
@@ -429,8 +445,13 @@
 
 
 def last_kernel(nxt, resid, small, singular, nxt_out, dirs_out, core_out, dirs, gram, wide, sem):
-    bulk = pltpu.make_async_copy(nxt, nxt_out, sem.at[0])
-    bulk.start()
+    bulk = [
+        pltpu.make_async_copy(nxt.at[e, f], nxt_out.at[e, f], sem.at[3 * e + f])
+        for e in range(3)
+        for f in range(3)
+    ]
+    for copy in bulk:
+        copy.start()
     gram[...] = jnp.transpose(jnp.broadcast_to(small[8:9, :], (128, 128)))
     low = [[None] * SNAPS for _ in range(SNAPS)]
     inv_diag = [None] * SNAPS
@@ -462,7 +483,7 @@
                 term = factors[j] * resid[j * ROWS + k * 8 : j * ROWS + k * 8 + 8, :]
                 acc = term if acc is None else acc + term
             dirs[i * ROWS + k * 8 : i * ROWS + k * 8 + 8, :] = acc
-    out = pltpu.make_async_copy(dirs, dirs_out, sem.at[1])
+    out = pltpu.make_async_copy(dirs, dirs_out, sem.at[9])
     out.start()
 
     row_id = lax.broadcasted_iota(jnp.int32, (RANK, 128), 0)
@@ -478,7 +499,8 @@
             block = jnp.where((row8 == i) & (lane8 == RANK + j), low[i][j], block)
     wide[RANK : RANK + 8, :] = block
     core_out[...] = jnp.transpose(wide[...])[0 : RANK + 8, 0 : RANK + 8]
-    bulk.wait()
+    for copy in bulk:
+        copy.wait()
     out.wait()
 
 
@@ -497,7 +519,7 @@
             vmem((SNAPS * ROWS, 128), f32),
             vmem((16, 128), f32),
         ),
-        in_specs=[in_hbm, in_hbm, in_hbm, in_hbm, pl.BlockSpec(memory_space=smem)],
+        in_specs=[in_hbm] * 5,
         out_specs=(in_vmem, in_vmem, in_vmem),
         scratch_shapes=[
             vmem((27, 8, 16, 512), f32),
@@ -505,18 +527,12 @@
             vmem((RANK * ROWS, 128), f32),
             vmem((SNAPS * ROWS, 128), f32),
             vmem((5, 16, 512), f32),
-            vmem((64, 16, 128), f32),
-            vmem((12, 16, 128), f32),
-            vmem((12, 8, 128), f32),
-            vmem((12, 8, 128), f32),
-            vmem((4, 16, 128), f32),
-            vmem((4, 16, 128), f32),
-            vmem((4, 8, 128), f32),
-            vmem((4, 8, 128), f32),
+            vmem((4, 20, 16, 128), f32),
             vmem((4, 128, 128), f32),
-            vmem((512, 128), f32),
-            vmem((2 * NDEV, 128), f32),
-            vmem((2 * NDEV, 128), f32),
+            vmem((4, 128, 128), f32),
+            vmem((2, 512, 128), f32),
+            vmem((4 * NDEV, 128), f32),
+            vmem((4 * NDEV, 128), f32),
             vmem((3, 3, 16, 512), f32),
             vmem((3, 3, 16, 512), f32),
             vmem((3, 3, 8, 1, 512), f32),
@@ -524,15 +540,14 @@
             vmem((4, 3, 1, 512), f32),
             vmem((SNAPS * RANK, 128), f32),
             vmem((8, 128), f32),
-            vmem((NDEV * 8, 128), f32),
+            vmem((NDEV * 4, 128), f32),
             vmem((8, 128), f32),
             vmem((NDEV, 128), f32),
             vmem((8, 128), f32),
             vmem((NDEV, 128), f32),
-            vmem((SNAPS * 128, 128), f32),
-            dma((11,)),
-            dma((3,)),
-            dma((3,)),
+            vmem((5 * 128, 128), f32),
+            smem((8,), jnp.int32),
+            dma((12,)),
             dma((8,)),
             dma((8,)),
             dma((4,)),
@@ -542,7 +557,7 @@
         compiler_params=pltpu.CompilerParams(
             collective_id=0, has_side_effects=True, vmem_limit_bytes=40 * 2**20
         ),
-    )(populations, solid, modes, earlier, age)
+    )(*(pltpu.with_memory_space_constraint(a, hbm) for a in (populations, solid, modes, earlier, age)))
     nxt_out, dirs, core = pl.pallas_call(
         last_kernel,
         out_shape=(
@@ -552,7 +567,7 @@
         ),
         in_specs=[in_vmem, in_vmem, in_vmem, in_vmem],
         out_specs=(in_hbm, in_hbm, in_vmem),
-        scratch_shapes=[vmem((SNAPS * ROWS, 128), f32), vmem((128, 128), f32), vmem((128, 128), f32), dma((2,))],
+        scratch_shapes=[vmem((SNAPS * ROWS, 128), f32), vmem((128, 128), f32), vmem((128, 128), f32), dma((10,))],
         compiler_params=pltpu.CompilerParams(vmem_limit_bytes=24 * 2**20),
     )(nxt, resid, small, singular.reshape(1, RANK))
     directions = dirs.reshape(SNAPS, 3, 32, 2, 128).transpose(0, 1, 3, 2, 4).reshape(SNAPS, 3, 2, 4096)

time: 55.6 us -> 41.8 us (0.75)
  Pallas kernels: 52.1 us -> 41.1 us
  local copies, waits for them, and re-layouts: 2.7 us -> 0.01 us
    pallas_call x1, Pallas kernels: 47.9 us -> 37.2 us  [per_device(): pl.pallas_call(main_kernel, out_shape=(vmem((3, 3, 3, 8, 16, 512), f32),...]
    unnamed x8 -> x2, local copies, waits for them, and re-layouts: 2.7 us -> 0.01 us
where the time goes in v1:
time: 41.8 us; the launch traced here: 41.7 us
  Pallas kernels  41.1 us (98%)
  between operations  0.66 us (2%)
    pallas_call x1, Pallas kernels, per_device(): pl.pallas_call(main_kernel, out_shape=(vmem((3, 3, 3, 8, 16, 512), f32),...  37.2 us
    pallas_call x1, Pallas kernels, per_device(): pl.pallas_call(last_kernel, out_shape=(jax.ShapeDtypeStruct((3, 3, 3, 8,...  3.85 us

profile of v1, /device:TPU:1, one launch (start us, length us, event | category | flops | bytes accessed | tf_op | source)
XLA Modules:
  0.0 41.7 jit_solution(7354726046477086689)
XLA Ops:
  0.6 0.0 copy-start
  0.6 37.2 %shard_map.85 = (f32[3,3,3,8,16,512]{5,4,3,2,1,0:T(8,128)S(1)}, f32[1536,128]{1,0:T(8,128)S(1)}, f32[16,128]{1,0:T(8,128)S(1)}) custom-call(f32[27,8,16,512]{3,2,1,0:T(8,128)} %pops_in.1, s32[8,16,512]{2,1,0:T(8,128)} %solid_in.1, f32[12288,128]{1,0:T(8,128)} %bitcast.18, f32[1344,128]{1,0:T(8,128)} %bitcast.19, s32[8]{0:T(128)} %age_in.1), custom_call_target="tpu_custom_call" | custom-call | tf_op jit(solution)/shard_map/pallas_call | solution.py:515
  37.9 0.0 copy-done
  37.9 3.9 %shard_map.86 = (f32[3,3,3,8,16,512]{5,4,3,2,1,0:T(8,128)}, f32[1536,128]{1,0:T(8,128)}, f32[72,72]{1,0:T(8,128)}) custom-call(f32[3,3,3,8,16,512]{5,4,3,2,1,0:T(8,128)S(1)} %get-tuple-element.9.nxt, f32[1536,128]{1,0:T(8,128)S(1)} %get-tuple-element.10.resid, f32[16,128]{1,0:T(8,128)S(1)} %get-tuple-element.11.small, f32[1,64]{1,0:T(1,128)S(1)} %bitcast.17), custom_call_target="tpu_custom_call" | custom-call | tf_op jit(solution)/shard_map/pallas_call | solution.py:561
Async XLA Ops:
  0.6 37.2 %copy-start = (f32[64]{0:T(128)S(1)}, f32[64]{0:T(128)}, u32[]{:S(2)}) copy-start(f32[64]{0:T(128)} %param.9) | copy-start | bytes 772

commit v2 on v1

--- a/solution.py
+++ b/solution.py
@@ -8,6 +8,7 @@
 from jax.sharding import PartitionSpec as P
 
 MESH = pl.DeviceIdType.MESH
+EARLY_FACES = 6
 HIGHEST = lax.Precision.HIGHEST
 omega_rate = 1.0 / 0.6
 keep_rate = 1.0 - omega_rate
@@ -112,28 +113,13 @@
     pops_in, solid_in, modes_in, recent_in, age_in,
     nxt, resid, small,
     pops, solid, modes, snaps, mo, sums, field, beyond, turned, parcel, arrived, xr_up, xr_dn, yr_up, yr_dn, corner,
-    stack, mine1, got1, mine2, got2, mine3, got3, spread,
-    age, load_sem, bulk_ssem, bulk_rsem, ex_ssem, ex_rsem, fix_sem,
+    stack, pair1, mine1, got1, mine2, got2, mine3, got3, spread,
+    age, load_sem, pair_sem, bulk_ssem, bulk_rsem, ex_ssem, ex_rsem, fix_sem,
 ):
     gx, gy = lax.axis_index("gx"), lax.axis_index("gy")
     me = gx * 4 + gy
     gx_up, gx_dn = lax.rem(gx + 1, 32), lax.rem(gx + 31, 32)
     gy_up, gy_dn = lax.rem(gy + 1, 4), lax.rem(gy + 3, 4)
-
-    solid_copy = pltpu.make_async_copy(solid_in, solid, load_sem.at[8])
-    solid_copy.start()
-
-    def plane_copy(x):
-        return pltpu.make_async_copy(pops_in.at[:, x], pops.at[:, x], load_sem.at[x])
-
-    for x in (7, 0, 1, 2, 3, 4, 5, 6):
-        plane_copy(x).start()
-    recent_copy = pltpu.make_async_copy(recent_in, snaps.at[pl.ds(ROWS, 7 * ROWS)], load_sem.at[9])
-    recent_copy.start()
-    modes_copy = pltpu.make_async_copy(modes_in, modes, load_sem.at[10])
-    modes_copy.start()
-    age_copy = pltpu.make_async_copy(age_in, age, load_sem.at[11])
-    age_copy.start()
 
     z_hi, x_at, y_at = lax.div(gx, 16), lax.rem(lax.div(gx, 4), 4), lax.rem(gx, 4)
     z_lo, core_at = lax.div(gy, 2), lax.rem(gy, 2)
@@ -151,10 +137,24 @@
                         if (jx, jy, jz, jl, jc) != (2, 2, 1, 0, 0):
                             peers.append((z_part[jz] + x_part[jx] + y_part[jy], lo_part[jl] + core_part[jc]))
 
+    solid_copy = pltpu.make_async_copy(solid_in, solid, load_sem.at[8])
+    solid_copy.start()
+
+    def plane_copy(x):
+        return pltpu.make_async_copy(pops_in.at[:, x], pops.at[:, x], load_sem.at[x])
+
+    for x in (7, 0, 1, 2, 3, 4, 5, 6):
+        plane_copy(x).start()
+    recent_copy = pltpu.make_async_copy(recent_in, snaps.at[pl.ds(ROWS, 7 * ROWS)], load_sem.at[9])
+    recent_copy.start()
+    modes_copy = pltpu.make_async_copy(modes_in, modes, load_sem.at[10])
+    modes_copy.start()
+    age_copy = pltpu.make_async_copy(age_in, age, load_sem.at[11])
+    age_copy.start()
+
     barrier = pltpu.get_barrier_semaphore()
     for peer in peers:
         pl.semaphore_signal(barrier, inc=1, device_id=peer, device_id_type=MESH)
-
     solid_copy.wait()
 
     def collide(k, carry):
@@ -208,16 +208,25 @@
             src_ref=src, dst_ref=dst, send_sem=ssem, recv_sem=rsem, device_id=to, device_id_type=MESH
         )
 
-    faces = [
-        remote(nxt.at[2, :, :, 0], xr_up, bulk_ssem.at[0], bulk_rsem.at[0], (gx_up, gy)),
-        remote(nxt.at[0, :, :, 7], xr_dn, bulk_ssem.at[1], bulk_rsem.at[1], (gx_dn, gy)),
-        remote(nxt.at[:, 2, :, :, pl.ds(0, 1)], yr_up, bulk_ssem.at[2], bulk_rsem.at[2], (gx, gy_up)),
-        remote(nxt.at[:, 0, :, :, pl.ds(15, 1)], yr_dn, bulk_ssem.at[3], bulk_rsem.at[3], (gx, gy_dn)),
-        remote(nxt.at[2, 2, :, 0, pl.ds(0, 1)], corner.at[0], bulk_ssem.at[4], bulk_rsem.at[4], (gx_up, gy_up)),
-        remote(nxt.at[2, 0, :, 0, pl.ds(15, 1)], corner.at[1], bulk_ssem.at[5], bulk_rsem.at[5], (gx_up, gy_dn)),
-        remote(nxt.at[0, 2, :, 7, pl.ds(0, 1)], corner.at[2], bulk_ssem.at[6], bulk_rsem.at[6], (gx_dn, gy_up)),
-        remote(nxt.at[0, 0, :, 7, pl.ds(15, 1)], corner.at[3], bulk_ssem.at[7], bulk_rsem.at[7], (gx_dn, gy_dn)),
+    def x_face(n, up):
+        e, plane, to, held = (2, 0, gx_up, xr_up) if up else (0, 7, gx_dn, xr_dn)
+        f, g = lax.div(n, 3), lax.rem(n, 3)
+        at = n if up else n + 9
+        return remote(nxt.at[e, f, g, plane], held.at[f, g], bulk_ssem.at[at], bulk_rsem.at[at], (to, gy))
+
+    others = [
+        remote(nxt.at[:, 2, :, :, pl.ds(0, 1)], yr_up, bulk_ssem.at[18], bulk_rsem.at[18], (gx, gy_up)),
+        remote(nxt.at[:, 0, :, :, pl.ds(15, 1)], yr_dn, bulk_ssem.at[19], bulk_rsem.at[19], (gx, gy_dn)),
+        remote(nxt.at[2, 2, :, 0, pl.ds(0, 1)], corner.at[0], bulk_ssem.at[20], bulk_rsem.at[20], (gx_up, gy_up)),
+        remote(nxt.at[2, 0, :, 0, pl.ds(15, 1)], corner.at[1], bulk_ssem.at[21], bulk_rsem.at[21], (gx_up, gy_dn)),
+        remote(nxt.at[0, 2, :, 7, pl.ds(0, 1)], corner.at[2], bulk_ssem.at[22], bulk_rsem.at[22], (gx_dn, gy_up)),
+        remote(nxt.at[0, 0, :, 7, pl.ds(15, 1)], corner.at[3], bulk_ssem.at[23], bulk_rsem.at[23], (gx_dn, gy_dn)),
     ]
+    def start_faces(first, last):
+        for n in range(first, last):
+            x_face(jnp.int32(n), True).start()
+            x_face(jnp.int32(n), False).start()
+
     def to_all(source, target, index, rows):
         place = target.at[pl.ds(me * rows, rows)]
         for peer in peers:
@@ -274,7 +283,14 @@
         mine1[r : r + 1, :] = row_totals(stack[r * 128 : (r + 1) * 128, :])[0:1]
 
 
-    to_all(lambda peer: mine1.at[pl.ds(0, 4)], got1, 1, 4)
+    other_core = gy + 1 - 2 * core_at
+    swap = remote(
+        mine1.at[pl.ds(2 - 2 * core_at, 2)], pair1.at[pl.ds(0, 2)], pair_sem.at[0], pair_sem.at[1], (gx, other_core)
+    )
+    swap.start()
+    swap.wait()
+    mine1[4:6, :] = jnp.where(core_at == 0, mine1[0:2, :], mine1[2:4, :]) + pair1[0:2, :]
+    to_all(lambda peer: mine1.at[pl.ds(4, 2)], got1, 1, 2)
 
     all_here(arrived, 0)
     lane = lax.broadcasted_iota(jnp.int32, (32, 128), 1)
@@ -320,7 +336,7 @@
             acc = None
             for k in range(24):
                 at = pl.ds(pl.multiple_of(base + n * ROWS + k * 8, 8), 8)
-                term = snaps[k * 8 : (k + 1) * 8, :] * modes[at, :]
+                term = fresh[k] * modes[at, :]
                 acc = term if acc is None else acc + term
             stack[pl.ds(block * 8 + n, 1), :] = jnp.sum(acc, axis=0, keepdims=True)
         return carry
@@ -330,12 +346,13 @@
     mine2[0:1, 0:RANK] = row_totals(stack[0:RANK, :])[0:1]
     to_all(lambda peer: mine2.at[pl.ds(0, 1)], got2, 2, 1)
 
-    for copy in faces:
+    start_faces(0, EARLY_FACES)
+    for copy in others:
         copy.start()
 
     all_here(got1, 1)
     total = got1[0:8, :]
-    for d in range(1, NDEV // 2):
+    for d in range(1, NDEV // 4):
         total = total + got1[d * 8 : (d + 1) * 8, :]
     total = (total[0:4] + total[4:8]) * (1.0 / TOTAL)
 
@@ -404,40 +421,48 @@
     mine3[...] = jnp.zeros((8, 128), jnp.float32)
     mine3[0:1, :] = row_totals(stack[0:128, :])[0:1]
     to_all(lambda peer: mine3.at[pl.ds(0, 1)], got3, 3, 1)
-    for copy in faces:
+    start_faces(EARLY_FACES, 9)
+    fixes = [
+        pltpu.make_async_copy(yr_up, nxt.at[:, 2, :, :, pl.ds(0, 1)], fix_sem.at[0]),
+        pltpu.make_async_copy(yr_dn, nxt.at[:, 0, :, :, pl.ds(15, 1)], fix_sem.at[1]),
+        pltpu.make_async_copy(xr_up, nxt.at[2, :, :, 0], fix_sem.at[2]),
+        pltpu.make_async_copy(xr_dn, nxt.at[0, :, :, 7], fix_sem.at[3]),
+        pltpu.make_async_copy(corner.at[0], nxt.at[2, 2, :, 0, pl.ds(0, 1)], fix_sem.at[4]),
+        pltpu.make_async_copy(corner.at[1], nxt.at[2, 0, :, 0, pl.ds(15, 1)], fix_sem.at[5]),
+        pltpu.make_async_copy(corner.at[2], nxt.at[0, 2, :, 7, pl.ds(0, 1)], fix_sem.at[6]),
+        pltpu.make_async_copy(corner.at[3], nxt.at[0, 0, :, 7, pl.ds(15, 1)], fix_sem.at[7]),
+    ]
+    for copy in others:
         copy.wait()
-    fixes = [
-        [
-            pltpu.make_async_copy(xr_up, nxt.at[2, :, :, 0], fix_sem.at[0]),
-            pltpu.make_async_copy(xr_dn, nxt.at[0, :, :, 7], fix_sem.at[1]),
-        ],
-        [
-            pltpu.make_async_copy(yr_up, nxt.at[:, 2, :, :, pl.ds(0, 1)], fix_sem.at[2]),
-            pltpu.make_async_copy(yr_dn, nxt.at[:, 0, :, :, pl.ds(15, 1)], fix_sem.at[3]),
-        ],
-        [
-            pltpu.make_async_copy(corner.at[0], nxt.at[2, 2, :, 0, pl.ds(0, 1)], fix_sem.at[4]),
-            pltpu.make_async_copy(corner.at[1], nxt.at[2, 0, :, 0, pl.ds(15, 1)], fix_sem.at[5]),
-            pltpu.make_async_copy(corner.at[2], nxt.at[0, 2, :, 7, pl.ds(0, 1)], fix_sem.at[6]),
-            pltpu.make_async_copy(corner.at[3], nxt.at[0, 0, :, 7, pl.ds(15, 1)], fix_sem.at[7]),
-        ],
-    ]
-    for copy in fixes[0]:
+
+    def face_sent(n, carry):
+        x_face(n, True).wait_send()
+        x_face(n, False).wait_send()
+        return carry
+
+    def face_here(n, carry):
+        x_face(n, True).wait_recv()
+        x_face(n, False).wait_recv()
+        return carry
+
+    lax.fori_loop(0, EARLY_FACES, face_sent, 0)
+    lax.fori_loop(0, EARLY_FACES, face_here, 0)
+    lax.fori_loop(EARLY_FACES, 9, face_sent, 0)
+    for copy in fixes[0:2]:
         copy.start()
-
-    for copy in fixes[0]:
+    for copy in fixes[0:2]:
         copy.wait()
-    for copy in fixes[1]:
+    lax.fori_loop(EARLY_FACES, 9, face_here, 0)
+    for copy in fixes[2:4]:
         copy.start()
-    for copy in fixes[1]:
+    for copy in fixes[2:4]:
         copy.wait()
-    for copy in fixes[2]:
+    for copy in fixes[4:8]:
         copy.start()
-
-    for copy in fixes[2]:
+    for copy in fixes[4:8]:
         copy.wait()
     all_sent(arrived, 0, 4)
-    all_sent(got1, 1, 4)
+    all_sent(got1, 1, 2)
     all_sent(got2, 2, 1)
     all_here(got3, 3)
     small[8:16, :] = jnp.broadcast_to(jnp.sum(got3[...], axis=0, keepdims=True) * (1.0 / TOTAL), (8, 128))
@@ -540,7 +565,8 @@
             vmem((4, 3, 1, 512), f32),
             vmem((SNAPS * RANK, 128), f32),
             vmem((8, 128), f32),
-            vmem((NDEV * 4, 128), f32),
+            vmem((8, 128), f32),
+            vmem((NDEV * 2, 128), f32),
             vmem((8, 128), f32),
             vmem((NDEV, 128), f32),
             vmem((8, 128), f32),
@@ -548,8 +574,9 @@
             vmem((5 * 128, 128), f32),
             smem((8,), jnp.int32),
             dma((12,)),
-            dma((8,)),
-            dma((8,)),
+            dma((2,)),
+            dma((24,)),
+            dma((24,)),
             dma((4,)),
             dma((4,)),
             dma((8,)),

time: 41.8 us -> 40.4 us (0.967)
  Pallas kernels: 41.1 us -> 39.6 us
    pallas_call x1, Pallas kernels: 37.2 us -> 35.7 us  [per_device(): pl.pallas_call(main_kernel, out_shape=(vmem((3, 3, 3, 8, 16, 512), f32),...]
where the time goes in v2:
time: 40.4 us; the launch traced here: 40.2 us
  Pallas kernels  39.6 us (98%)
  between operations  0.66 us (2%)
    pallas_call x1, Pallas kernels, per_device(): pl.pallas_call(main_kernel, out_shape=(vmem((3, 3, 3, 8, 16, 512), f32),...  35.7 us
    pallas_call x1, Pallas kernels, per_device(): pl.pallas_call(last_kernel, out_shape=(jax.ShapeDtypeStruct((3, 3, 3, 8,...  3.85 us

profile of v2, /device:TPU:1, one launch (start us, length us, event | category | flops | bytes accessed | tf_op | source)
XLA Modules:
  0.0 40.2 jit_solution(5676854585795799985)
XLA Ops:
  0.6 0.0 copy-start
  0.6 35.7 %shard_map.85 = (f32[3,3,3,8,16,512]{5,4,3,2,1,0:T(8,128)S(1)}, f32[1536,128]{1,0:T(8,128)S(1)}, f32[16,128]{1,0:T(8,128)S(1)}) custom-call(f32[27,8,16,512]{3,2,1,0:T(8,128)} %pops_in.1, s32[8,16,512]{2,1,0:T(8,128)} %solid_in.1, f32[12288,128]{1,0:T(8,128)} %bitcast.18, f32[1344,128]{1,0:T(8,128)} %bitcast.19, s32[8]{0:T(128)} %age_in.1), custom_call_target="tpu_custom_call" | custom-call | tf_op jit(solution)/shard_map/pallas_call | solution.py:540
  36.4 0.0 copy-done
  36.4 3.9 %shard_map.86 = (f32[3,3,3,8,16,512]{5,4,3,2,1,0:T(8,128)}, f32[1536,128]{1,0:T(8,128)}, f32[72,72]{1,0:T(8,128)}) custom-call(f32[3,3,3,8,16,512]{5,4,3,2,1,0:T(8,128)S(1)} %get-tuple-element.9.nxt, f32[1536,128]{1,0:T(8,128)S(1)} %get-tuple-element.10.resid, f32[16,128]{1,0:T(8,128)S(1)} %get-tuple-element.11.small, f32[1,64]{1,0:T(1,128)S(1)} %bitcast.17), custom_call_target="tpu_custom_call" | custom-call | tf_op jit(solution)/shard_map/pallas_call | solution.py:588
Async XLA Ops:
  0.6 35.8 %copy-start = (f32[64]{0:T(128)S(1)}, f32[64]{0:T(128)}, u32[]{:S(2)}) copy-start(f32[64]{0:T(128)} %param.9) | copy-start | bytes 772

commit v3 on v2

--- a/solution.py
+++ b/solution.py
@@ -9,7 +9,6 @@
 
 MESH = pl.DeviceIdType.MESH
 EARLY_FACES = 6
-HIGHEST = lax.Precision.HIGHEST
 omega_rate = 1.0 / 0.6
 keep_rate = 1.0 - omega_rate
 vel_gain = 50.0
@@ -271,16 +270,13 @@
         return carry
 
     lax.fori_loop(0, RANK // 4, project, 0)
-    ones = jnp.ones((8, 128), jnp.float32)
 
     def row_totals(block):
-        return lax.dot_general(
-            ones, block, (((1,), (1,)), ((), ())), precision=HIGHEST, preferred_element_type=jnp.float32
-        )
+        return jnp.sum(jnp.transpose(block), axis=0, keepdims=True)
 
     stack[0:RANK, :] = jnp.zeros((RANK, 128), jnp.float32)
     for r in range(4):
-        mine1[r : r + 1, :] = row_totals(stack[r * 128 : (r + 1) * 128, :])[0:1]
+        mine1[r : r + 1, :] = row_totals(stack[r * 128 : (r + 1) * 128, :])
 
 
     other_core = gy + 1 - 2 * core_at
@@ -343,7 +339,7 @@
 
     lax.fori_loop(0, RANK // 8, project_fresh, 0)
     mine2[...] = jnp.zeros((8, 128), jnp.float32)
-    mine2[0:1, 0:RANK] = row_totals(stack[0:RANK, :])[0:1]
+    mine2[0:1, :] = row_totals(stack[0:128, :])
     to_all(lambda peer: mine2.at[pl.ds(0, 1)], got2, 2, 1)
 
     start_faces(0, EARLY_FACES)
@@ -419,7 +415,7 @@
     lax.fori_loop(0, ROWS // 64, subtract_fresh, 0)
     inner_products([(i, 0) for i in range(SNAPS)])
     mine3[...] = jnp.zeros((8, 128), jnp.float32)
-    mine3[0:1, :] = row_totals(stack[0:128, :])[0:1]
+    mine3[0:1, :] = row_totals(stack[0:128, :])
     to_all(lambda peer: mine3.at[pl.ds(0, 1)], got3, 3, 1)
     start_faces(EARLY_FACES, 9)
     fixes = [

time: 40.4 us -> 39.9 us (0.988)
    pallas_call x1, Pallas kernels: 35.7 us -> 35.3 us  [per_device(): pl.pallas_call(main_kernel, out_shape=(vmem((3, 3, 3, 8, 16, 512), f32),...]
where the time goes in v3:
time: 39.9 us; the launch traced here: 39.8 us
  Pallas kernels  39.2 us (98%)
  between operations  0.66 us (2%)
    pallas_call x1, Pallas kernels, per_device(): pl.pallas_call(main_kernel, out_shape=(vmem((3, 3, 3, 8, 16, 512), f32),...  35.3 us
    pallas_call x1, Pallas kernels, per_device(): pl.pallas_call(last_kernel, out_shape=(jax.ShapeDtypeStruct((3, 3, 3, 8,...  3.85 us

profile of v3, /device:TPU:1, one launch (start us, length us, event | category | flops | bytes accessed | tf_op | source)
XLA Modules:
  0.0 39.8 jit_solution(4888176754995713032)
XLA Ops:
  0.6 0.0 copy-start
  0.6 35.3 %shard_map.85 = (f32[3,3,3,8,16,512]{5,4,3,2,1,0:T(8,128)S(1)}, f32[1536,128]{1,0:T(8,128)S(1)}, f32[16,128]{1,0:T(8,128)S(1)}) custom-call(f32[27,8,16,512]{3,2,1,0:T(8,128)} %pops_in.1, s32[8,16,512]{2,1,0:T(8,128)} %solid_in.1, f32[12288,128]{1,0:T(8,128)} %bitcast.18, f32[1344,128]{1,0:T(8,128)} %bitcast.19, s32[8]{0:T(128)} %age_in.1), custom_call_target="tpu_custom_call" | custom-call | tf_op jit(solution)/shard_map/pallas_call | solution.py:536
  36.0 0.0 copy-done
  36.0 3.9 %shard_map.86 = (f32[3,3,3,8,16,512]{5,4,3,2,1,0:T(8,128)}, f32[1536,128]{1,0:T(8,128)}, f32[72,72]{1,0:T(8,128)}) custom-call(f32[3,3,3,8,16,512]{5,4,3,2,1,0:T(8,128)S(1)} %get-tuple-element.9.nxt, f32[1536,128]{1,0:T(8,128)S(1)} %get-tuple-element.10.resid, f32[16,128]{1,0:T(8,128)S(1)} %get-tuple-element.11.small, f32[1,64]{1,0:T(1,128)S(1)} %bitcast.17), custom_call_target="tpu_custom_call" | custom-call | tf_op jit(solution)/shard_map/pallas_call | solution.py:584
Async XLA Ops:
  0.6 35.3 %copy-start = (f32[64]{0:T(128)S(1)}, f32[64]{0:T(128)}, u32[]{:S(2)}) copy-start(f32[64]{0:T(128)} %param.9) | copy-start | bytes 772

commit v4 on v3

--- a/solution.py
+++ b/solution.py
@@ -410,10 +410,19 @@
                 acc[n] = acc[n] - c * modes[pl.ds(pl.multiple_of(base + m * ROWS + n * 8, 8), 8), :]
         for n in range(8):
             resid[pl.ds(pl.multiple_of(base + n * 8, 8), 8), :] = acc[n]
-        return carry
-
-    lax.fori_loop(0, ROWS // 64, subtract_fresh, 0)
-    inner_products([(i, 0) for i in range(SNAPS)])
+        out = []
+        for i in range(SNAPS):
+            product = carry[i]
+            for n in range(8):
+                at = pl.ds(pl.multiple_of(base + i * ROWS + n * 8, 8), 8)
+                product = product + acc[n] * (resid[at, :] if i else acc[n])
+            out.append(product)
+        return tuple(out)
+
+    zero = jnp.zeros((8, 128), jnp.float32)
+    products = lax.fori_loop(0, ROWS // 64, subtract_fresh, (zero,) * SNAPS)
+    for i in range(SNAPS):
+        stack[i * 8 : i * 8 + 1, :] = jnp.sum(products[i], axis=0, keepdims=True)
     mine3[...] = jnp.zeros((8, 128), jnp.float32)
     mine3[0:1, :] = row_totals(stack[0:128, :])
     to_all(lambda peer: mine3.at[pl.ds(0, 1)], got3, 3, 1)

time: 39.9 us -> 40.1 us (level)
  no operation moved by 1% of the time
where the time goes in v4:
time: 40.1 us; the launch traced here: 40 us
  Pallas kernels  39.3 us (98%)
  between operations  0.66 us (2%)
    pallas_call x1, Pallas kernels, per_device(): pl.pallas_call(main_kernel, out_shape=(vmem((3, 3, 3, 8, 16, 512), f32),...  35.5 us
    pallas_call x1, Pallas kernels, per_device(): pl.pallas_call(last_kernel, out_shape=(jax.ShapeDtypeStruct((3, 3, 3, 8,...  3.85 us

profile of v4, /device:TPU:1, one launch (start us, length us, event | category | flops | bytes accessed | tf_op | source)
XLA Modules:
  0.0 40.0 jit_solution(2931620516888148051)
XLA Ops:
  0.6 0.0 copy-start
  0.6 35.5 %shard_map.85 = (f32[3,3,3,8,16,512]{5,4,3,2,1,0:T(8,128)S(1)}, f32[1536,128]{1,0:T(8,128)S(1)}, f32[16,128]{1,0:T(8,128)S(1)}) custom-call(f32[27,8,16,512]{3,2,1,0:T(8,128)} %pops_in.1, s32[8,16,512]{2,1,0:T(8,128)} %solid_in.1, f32[12288,128]{1,0:T(8,128)} %bitcast.18, f32[1344,128]{1,0:T(8,128)} %bitcast.19, s32[8]{0:T(128)} %age_in.1), custom_call_target="tpu_custom_call" | custom-call | tf_op jit(solution)/shard_map/pallas_call | solution.py:545
  36.1 0.0 copy-done
  36.1 3.9 %shard_map.86 = (f32[3,3,3,8,16,512]{5,4,3,2,1,0:T(8,128)}, f32[1536,128]{1,0:T(8,128)}, f32[72,72]{1,0:T(8,128)}) custom-call(f32[3,3,3,8,16,512]{5,4,3,2,1,0:T(8,128)S(1)} %get-tuple-element.9.nxt, f32[1536,128]{1,0:T(8,128)S(1)} %get-tuple-element.10.resid, f32[16,128]{1,0:T(8,128)S(1)} %get-tuple-element.11.small, f32[1,64]{1,0:T(1,128)S(1)} %bitcast.17), custom_call_target="tpu_custom_call" | custom-call | tf_op jit(solution)/shard_map/pallas_call | solution.py:593
Async XLA Ops:
  0.6 35.5 %copy-start = (f32[64]{0:T(128)S(1)}, f32[64]{0:T(128)}, u32[]{:S(2)}) copy-start(f32[64]{0:T(128)} %param.9) | copy-start | bytes 772
